TPU v7x, 256 devices: a whole 4x4x8 slice. The times are simulated.
256 devices in a mesh: frames: 8 (over x_hi, y), feat: 32 (over z, x_lo, core).
Axes of the slice: x: 4 (x_hi: 2, x_lo: 2; x = x_hi * 2 + x_lo), y: 4, z: 8, core: 2. Of those that a mesh axis runs over, the one named last changes fastest.
Arguments:
- frames_in: bfloat16 [8192, 440], P(('frames', 'feat')), may hold values from -8 to 8
- labels: int32 [8192], P('frames'), may hold values from 0 to 146
- projection: bfloat16 [440, 131072], P(None, 'feat'), may hold values from -0.25 to 0.25
- kernel_scale: float32 [32], P('feat'), may hold values from 0.5 to 3
- shift: float32 [131072], P('feat'), may hold values from -3.140625 to 3.140625
- weights: float32 [147, 131072], P(None, 'feat'), may hold values from -100 to 100
- readout: float32 [147, 440], replicated, may hold values from -8 to 8
Outputs:
- new_weights: float32 [147, 131072], P(None, ('feat', 'frames'))
- new_readout: float32 [147, 440], replicated
All inputs are finite; a program needn't handle non-finite values.
Results may differ from a plain program's by a relative error of at most 0.0075.
Values may be sent and summed in bfloat16 or wider, within the bound.
A program may use at most 64 MiB of HBM per device.

v0:
```python
import math

import jax
import jax.numpy as jnp
from jax import lax
from jax.sharding import PartitionSpec as P


def class_residual(scores, labels):
    probs = jax.nn.softmax(scores, axis=0)
    onehot = (jnp.arange(scores.shape[0])[:, None] == labels[None, :]).astype(jnp.float32)
    return (probs - onehot).astype(jnp.bfloat16)


def body(frames_in, labels, projection, kernel_scale, shift, weights, readout):
    n_feat = lax.axis_size("feat")
    n_frames = lax.axis_size("frames")
    rows = frames_in.shape[0]
    group_tok = labels.shape[0]
    batch = group_tok * n_frames
    feat_total = weights.shape[1] * n_feat
    member = lax.axis_index("feat")
    weights_low = weights.astype(jnp.bfloat16)
    linear_own = jnp.dot(readout, frames_in.astype(jnp.float32).T, precision=lax.Precision.HIGHEST)
    phase = (
        jnp.dot(
            lax.all_gather(frames_in, "feat", axis=0, tiled=True),
            projection,
            preferred_element_type=jnp.float32,
        )
        * kernel_scale[0]
        + shift
    )
    features = (math.sqrt(2.0) * jnp.cos(phase)).astype(jnp.bfloat16)
    partial_value = lax.dot_general(
        weights_low, features, (((1,), (1,)), ((), ())), preferred_element_type=jnp.float32
    )
    partial_value = partial_value / math.sqrt(feat_total)
    own_block = lax.dynamic_slice_in_dim(partial_value, member * rows, rows, 1) + linear_own
    partial_value = lax.dynamic_update_slice_in_dim(partial_value, own_block, member * rows, 1)
    scores = lax.psum(partial_value, "feat")
    residual = class_residual(scores, labels)
    residual_own = lax.dynamic_slice_in_dim(residual, member * rows, rows, 1)
    gradient = jnp.dot(residual, features, preferred_element_type=jnp.float32)
    readout_grad = lax.psum(
        jnp.dot(residual_own, frames_in, preferred_element_type=jnp.float32), ("frames", "feat")
    )
    new_readout = readout - 3.0 / math.sqrt(batch) * readout_grad
    rate = 5.0 / math.sqrt(batch)
    limit = 1.5 * math.sqrt(weights.shape[1] * weights.shape[0])
    columns = weights.shape[1] // n_frames
    frame_index = lax.axis_index("frames")
    total = lax.psum(gradient.astype(jnp.bfloat16), "frames").astype(jnp.float32)
    stepped = weights - rate * total
    trimmed = jnp.sign(stepped) * jnp.maximum(jnp.abs(stepped) - 1.0, 0.0)
    group_norm = jnp.sqrt(jnp.sum(trimmed * trimmed) + 1e-06)
    trimmed = lax.dynamic_slice_in_dim(trimmed, frame_index * columns, columns, 1)
    new_weights = trimmed * jnp.maximum(0.0, 1.0 - limit / group_norm)
    return (new_weights, new_readout)


def solution(mesh):
    return jax.shard_map(
        body,
        mesh=mesh,
        in_specs=(
            P(("frames", "feat"), None),
            P("frames"),
            P(None, "feat"),
            P("feat"),
            P("feat"),
            P(None, "feat"),
            P(),
        ),
        out_specs=(P(None, ("feat", "frames")), P()),
        check_vma=False,
    )
```

profile of v0, /device:TPU:1, one launch (start us, length us, event | category | flops | bytes accessed | tf_op | source)
XLA Modules:
  0.0 684.4 jit_solution(16733650141800510444)
XLA Ops:
  7.2 0.0 all-reduce.4.cloned.1.call-start
  7.9 41.6 %all_gather.3 = bf16[1024,440]{1,0:T(8,128)(2,1)S(1)} all-gather(bf16[32,440]{1,0:T(8,128)(2,1)} %param.7), channel_id=1, replica_groups=mesh['frames'=8,'feat'=32] {'feat'}, dimensions={0}, use_global_device_ids=true | all-gather | bytes 929280 | tf_op jit(solution)/shard_map/all_gather | solution.py:27
  49.4 59.5 %multiply_convert_fusion = bf16[1024,4096]{1,0:T(8,128)(2,1)S(1)} fusion(bf16[1024,440]{1,0:T(8,128)(2,1)S(1)} %all_gather.3, bf16[440,4096]{1,0:T(8,128)(2,1)} %param.9, f32[4096]{0:T(1024)} %param.11, f32[]{:T(128)} %bitcast.12), kind=kOutput, calls=%fused_computation | convolution fusion | flops 3707764736 | bytes 12910596 | tf_op jit(solution)/shard_map/dot_general | solution.py:26
  109.0 2.9 convolution_multiply_fusion
  111.9 0.3 copy-done
  112.2 0.3 convolution_add_fusion
  112.4 1.0 dynamic_update_slice.3
  113.4 0.9 copy-done.2
  114.3 0.0 all-reduce.4.cloned.1.call-update
  114.3 0.0 all-reduce.8.cloned.1.call-start
  114.4 213.2 %all-reduce.4.cloned.1.call-done = f32[147,1024]{1,0:T(8,128)} async-done(((f32[147,1024]{1,0:T(8,128)}), f32[147,1024]{1,0:T(8,128)}) %all-reduce.4.cloned.1.call-update) | async-done | bytes 602128 | tf_op jit(solution)/shard_map/psum | solution.py:41
  327.6 1.1 reduce_max.9
  328.7 1.2 fusion.1
  329.9 1.2 subtract_convert_fusion
  331.2 1.0 fusion.2
  332.1 0.0 all-reduce.8.cloned.1.call-update
  332.2 0.0 all-reduce.6.cloned.1.call-start
  332.2 6.0 convolution_convert_fusion
  338.2 0.0 all-reduce.6.cloned.1.call-update
  338.2 244.4 %all-reduce.8.cloned.1.call-done = f32[147,440]{1,0:T(8,128)} async-done(((f32[147,440]{1,0:T(8,128)}), f32[147,440]{1,0:T(8,128)}) %all-reduce.8.cloned.1.call-update) | async-done | bytes 258736 | tf_op jit(solution)/shard_map/psum | solution.py:45
  582.6 1.7 multiply_subtract_fusion
  584.4 86.5 %all-reduce.6.cloned.1.call-done = bf16[147,4096]{1,0:T(8,128)(2,1)} async-done(((bf16[147,4096]{1,0:T(8,128)(2,1)}), bf16[147,4096]{1,0:T(8,128)(2,1)}) %all-reduce.6.cloned.1.call-update) | async-done | bytes 1204240 | tf_op jit(solution)/shard_map/psum | solution.py:53
  670.9 4.6 multiply_reduce_fusion
  676.2 1.7 dynamic-slice_multiply_fusion
  (10 shorter events, 0.0 us)
Async XLA Ops:
  7.2 320.4 %all-reduce.4.cloned.1.call-start = ((), (), s32[]{:S(2)}) async-start(), calls=%async_computation | async-start | bytes 1245184 | tf_op jit(solution)/shard_map/psum | solution.py:41
  49.4 59.5 %copy-start.1 = (f32[147,4096]{1,0:T(8,128)S(1)}, f32[147,4096]{1,0:T(8,128)}, u32[]{:S(2)}) copy-start(f32[147,4096]{1,0:T(8,128)} %param.12) | copy-start | bytes 7225348
  108.9 3.2 copy-start
  108.9 3.2 copy-start.3
  108.9 3.2 copy-start.4
  112.2 217.8 %copy-start.5 = (s32[1024]{0:T(1024)S(1)}, s32[1024]{0:T(1024)}, u32[]{:S(2)}) copy-start(s32[1024]{0:T(1024)} %param.8) | copy-start | bytes 12292
  113.4 0.9 copy-start.2
  114.3 468.3 %all-reduce.8.cloned.1.call-start = ((), (), s32[]{:S(2)}) async-start(), calls=%async_computation.2 | async-start | bytes 622592 | tf_op jit(solution)/shard_map/psum | solution.py:45
  332.2 338.7 %all-reduce.6.cloned.1.call-start = ((), (), s32[]{:S(2)}) async-start(), calls=%async_computation.1 | async-start | bytes 2490368 | tf_op jit(solution)/shard_map/psum | solution.py:53
Sparse Core Ops, SparseCore 0:
  114.4 213.1 all-reduce.3
  334.6 247.9 all-reduce.7
  585.5 85.3 all-reduce.5
where the time goes:
time: 689 us; the launch traced here: 684 us
  waiting for transfers between devices  544 us (79%)
  matrix products  69.6 us (10%)
  blocking collectives  41.6 us (6%)
  between operations  15.2 us (2%)
  other arithmetic  11.6 us (2%)
    psum x1, waiting for transfers between devices, body(): lax.psum(jnp.dot(residual_own, frames_in, preferred_element_type=jnp.floa...  244 us
    psum x1, waiting for transfers between devices, body(): scores = lax.psum(partial_value, 'feat')  213 us
    psum x1, waiting for transfers between devices, body(): lax.psum(gradient.astype(jnp.bfloat16), 'frames').astype(jnp.float32)  86.5 us
    dot_general x1, matrix products, body(): jnp.dot(lax.all_gather(frames_in, 'feat', axis=0, tiled=True), projection...  59.5 us
    all_gather x1, blocking collectives, body(): lax.all_gather(frames_in, 'feat', axis=0, tiled=True)  41.6 us
  transfers between devices with their start and end apart: 3, of which 3 were waited for; matrix products, arithmetic and copies ran while one was open for 1% of the time, Pallas kernels for 0%

commit v1 on v0

v1 whole, which is shorter than its diff:
```python
import functools
import math

import jax
import jax.numpy as jnp
from jax import lax
from jax.experimental import pallas as pl
from jax.experimental.pallas import tpu as pltpu
from jax.sharding import PartitionSpec as P

MESH = pl.DeviceIdType.MESH
F32, BF16 = jnp.float32, jnp.bfloat16
LANES = 256
ROWS = 160
NB = 256

OFFS = (0, 1, -1, 2, -2, 3, -3, 4)
MIRROR = tuple(OFFS.index(-d) if -d in OFFS else OFFS.index(d) for d in OFFS)
CHUNKS = ((0, 1), (1, 3), (3, 5), (5, 7), (7, 8))

COS = (1.4142124652862549, -27.91513442993164, 91.82299041748047, -120.59228515625, 83.1423110961914, -29.799043655395508)


def features_of(product, scale, shift):
    turns = product * scale + shift
    r = turns - jnp.round(turns)
    u = r * r
    acc = COS[-1] * u + COS[-2]
    for c in COS[-3::-1]:
        acc = acc * u + c
    return acc.astype(BF16)


def kernel(
    batch, feat_total, classes,
    scale_ref, x_hbm, proj_hbm, w_hbm, labels_ref, shift_ref, readout_ref,
    out_ref, grad_out_ref,
    x_own, proj, w, w_low, x_all, feats, lab, kept, pair_out, pair_in, sum_out, sum_in,
    res_all, res_t, grad_out, grad_in, ro_t, ro_out, ro_in, ro_own, norm_out, norm_in,
    local_sem, x_send, x_recv, pair_send, pair_recv, sum_send, sum_recv, res_send, res_recv,
    grad_send, grad_recv, ro_send, ro_recv, all_send, all_recv, norm_send, norm_recv,
):
    me = lax.axis_index("feat")
    group = lax.axis_index("frames")
    z, q = me // 4, me % 4
    xh, y = group // 4, group % 4
    q_sib = q + 1 - 2 * (q % 2)
    q_x = (q + 2) % 4

    def feat_dev(d, qq):
        return {"feat": ((z + d + 8) % 8) * 4 + qq}

    def frame_dev(k):
        dx, dy = k // 4, k % 4
        return ((xh + dx) % 2) * 4 + (y + dy) % 4

    sibling, neighbour = feat_dev(0, q_sib), feat_dev(0, q_x)
    sends = []

    def send(src, dst, ssem, rsem, dev):
        copy = pltpu.make_async_remote_copy(
            src_ref=src, dst_ref=dst, send_sem=ssem, recv_sem=rsem, device_id=dev, device_id_type=MESH
        )
        copy.start()
        sends.append(copy)

    def arrived(ref, rsem):
        pltpu.make_async_remote_copy(
            src_ref=ref, dst_ref=ref, send_sem=x_send.at[0], recv_sem=rsem, device_id=sibling, device_id_type=MESH
        ).wait_recv()

    copy_x = pltpu.make_async_copy(x_hbm, x_own, local_sem.at[0])
    copy_p = pltpu.make_async_copy(proj_hbm, proj, local_sem.at[1])
    copy_w = pltpu.make_async_copy(w_hbm, w, local_sem.at[2])
    copy_x.start()
    copy_p.start()
    copy_w.start()

    barrier = pltpu.get_barrier_semaphore()
    partners = [feat_dev(d, q) for d in OFFS[1:]] + [feat_dev(d, q_x) for d in OFFS] + [sibling]
    partners += [{"frames": frame_dev(k)} for k in range(1, 8)]
    for dev in partners:
        pl.semaphore_signal(barrier, inc=1, device_id=dev, device_id_type=MESH)
    copy_x.wait()
    x_all[0, 0] = x_own[...]
    pl.semaphore_wait(barrier, len(partners))

    def gather_start(buf, ss, rs):
        for s in (7, 6, 5, 4, 3, 2, 1):
            m = MIRROR[s]
            send(buf.at[0, 0], buf.at[m, 0], ss.at[s], rs.at[m, 0], feat_dev(OFFS[s], q))
        gather_local(buf, ss, rs, 0, False)

    def gather_local(buf, ss, rs, s, wait=True):
        if wait:
            arrived(buf.at[s, 0], rs.at[s, 0])
        send(buf.at[s, 0], buf.at[s, 2], ss.at[8 + s], rs.at[s, 2], neighbour)
        send(buf.at[s, 0], buf.at[s, 1], ss.at[16 + s], rs.at[s, 1], sibling)

    def gather_last(buf, ss, rs, s):
        arrived(buf.at[s, 2], rs.at[s, 2])
        send(buf.at[s, 2], buf.at[s, 3], ss.at[24 + s], rs.at[s, 3], sibling)

    def gather_wait(buf, rs, s):
        arrived(buf.at[s, 1], rs.at[s, 1])
        arrived(buf.at[s, 3], rs.at[s, 3])

    gather_start(x_all, x_send, x_recv)

    w_low[144:LANES, :] = jnp.zeros((LANES - 144, w_low.shape[1]), BF16)
    copy_w.wait()
    w_low[0:classes, :] = w[...].astype(BF16)
    ro = readout_ref[...]
    ro_hi = ro.astype(BF16)
    rest = ro - ro_hi.astype(F32)
    ro_mid = rest.astype(BF16)
    ro_lo = (rest - ro_mid.astype(F32)).astype(BF16)
    nt = (((1,), (1,)), ((), ()))
    x0 = x_own[...]
    linear = (
        lax.dot_general(x0, ro_hi, nt, preferred_element_type=F32)
        + lax.dot_general(x0, ro_mid, nt, preferred_element_type=F32)
        + lax.dot_general(x0, ro_lo, nt, preferred_element_type=F32)
    )
    row = jnp.broadcast_to(labels_ref[pl.ds(z, 1), :].astype(F32), (128, 128))
    lab[...] = row.T
    copy_p.wait()

    turn = 1.0 / (2.0 * math.pi)
    scale = scale_ref[0] * turn

    def half(chunk, first):
        lo, hi = chunk
        n = (hi - lo) * 128
        xs = x_all[lo:hi].reshape(n, x_all.shape[-1])

        def block(j, carry):
            cols = pl.ds(pl.multiple_of(j * NB, NB), NB)
            product = jnp.dot(xs, proj[:, cols], preferred_element_type=F32)
            feats[lo * 128 : hi * 128, cols] = features_of(product, scale, shift_ref[:, cols] * turn)
            return carry

        count = feats.shape[1] // NB // 2
        lax.fori_loop(first * count, (first + 1) * count, block, 0, unroll=True)

    def scores(chunk):
        lo, hi = chunk
        part = lax.dot_general(feats[lo * 128 : hi * 128, :], w_low[...], nt, preferred_element_type=F32)
        part = part.reshape(hi - lo, 4, 32, LANES)
        for s in range(lo, hi):
            for j in range(2):
                kept[s, j] = part[s - lo, 2 * j]
                pair_out[s, j] = part[s - lo, 2 * j + 1].astype(BF16)
            send(pair_out.at[s], pair_in.at[s], pair_send.at[s], pair_recv.at[s], sibling)

    def pass_on(chunk):
        for s in range(*chunk):
            arrived(pair_in.at[s], pair_recv.at[s])
            m = MIRROR[s]
            for j in range(2):
                total = kept[s, j] + pair_in[s, j].astype(F32)
                if s == 0 and j == 0:
                    kept[0, 0] = total
                else:
                    sum_out[s, j] = total.astype(BF16)
                    dev = feat_dev(OFFS[s], q_x if j else q)
                    send(sum_out.at[s, j], sum_in.at[m, j], sum_send.at[s, j], sum_recv.at[m, j], dev)

    for index, chunk in enumerate(CHUNKS):
        later = CHUNKS[index + 1] if index + 1 < len(CHUNKS) else (0, 0)
        if index == 0:
            gather_last(x_all, x_send, x_recv, 0)
        for s in range(*later):
            gather_local(x_all, x_send, x_recv, s)
        for s in range(*chunk):
            gather_wait(x_all, x_recv, s)
        half(chunk, 0)
        for s in range(*later):
            gather_last(x_all, x_send, x_recv, s)
        if index:
            pass_on(CHUNKS[index - 1])
        half(chunk, 1)
        scores(chunk)
    pass_on(CHUNKS[-1])

    total = kept[0, 0]
    for s in range(8):
        for j in range(2):
            if s or j:
                arrived(sum_in.at[s, j], sum_recv.at[s, j])
                total = total + sum_in[s, j].astype(F32)
    lanes = lax.broadcasted_iota(jnp.int32, (32, LANES), 1)
    inside = lanes < classes
    linear = jnp.concatenate([linear, jnp.zeros((32, LANES - classes), F32)], axis=1)
    value = total * (1.0 / math.sqrt(feat_total)) + linear
    value = jnp.where(inside, value, -1e30)
    value = jnp.exp(value - jnp.max(value, axis=1, keepdims=True))
    probs = value / jnp.sum(value, axis=1, keepdims=True)
    mine = lab[pl.ds(pl.multiple_of(q * 32, 32), 32), :]
    mine = jnp.concatenate([mine, mine], axis=1)
    res_all[0, 0] = jnp.where(lanes.astype(F32) == mine, probs - 1.0, probs).astype(BF16)

    gather_start(res_all, res_send, res_recv)
    gather_last(res_all, res_send, res_recv, 0)
    for s in range(1, 8):
        gather_local(res_all, res_send, res_recv, s)
    for s in range(1, 8):
        gather_last(res_all, res_send, res_recv, s)
    for s in range(8):
        gather_wait(res_all, res_recv, s)

    res_t[...] = res_all[...].reshape(1024, LANES).T[:ROWS]
    cols_each = out_ref.shape[1]

    def grad_block(k):
        cols = pl.ds(pl.multiple_of(frame_dev(k) * cols_each, cols_each), cols_each)
        return jnp.dot(res_t[...], feats[:, cols], preferred_element_type=F32)

    back = [0] + [(k // 4) * 4 + (4 - k % 4) % 4 for k in range(1, 8)]
    for k in (6, 5, 7, 2, 4, 1, 3):
        grad_out[k] = grad_block(k).astype(BF16)
        b = back[k]
        send(grad_out.at[k], grad_in.at[b], grad_send.at[k], grad_recv.at[b], {"frames": frame_dev(k)})

    ro_grad = jnp.dot(res_t[...], x_all[...].reshape(1024, x_all.shape[-1]), preferred_element_type=F32)
    ro_t[...] = jnp.zeros_like(ro_t)
    ro_t[0 : ro_grad.shape[1], 0:ROWS] = ro_grad.T
    own_rows = pl.ds(pl.multiple_of(me * 16, 16), 16)
    ro_out[...] = ro_t[own_rows, :].astype(BF16)
    for k in range(1, 8):
        b = back[k]
        send(ro_out, ro_in.at[b], ro_send.at[k], ro_recv.at[b], {"frames": frame_dev(k)})
    own_grad = grad_block(0)
    total = ro_t[own_rows, :]
    for k in range(1, 8):
        arrived(ro_in.at[k], ro_recv.at[k])
        total = total + ro_in[k].astype(F32)
    ro_own[0, 0] = total.astype(BF16)
    gather_start(ro_own, all_send, all_recv)
    gather_last(ro_own, all_send, all_recv, 0)
    for s in range(1, 8):
        gather_local(ro_own, all_send, all_recv, s)
    for s in range(1, 8):
        gather_last(ro_own, all_send, all_recv, s)
    for s in range(8):
        gather_wait(ro_own, all_recv, s)
    for s in range(8):
        for r, qq in enumerate((q, q_sib, q_x, 3 - q)):
            at = (((z + OFFS[s] + 8) % 8) * 4 + qq) * 16
            grad_out_ref[pl.ds(pl.multiple_of(at, 16), 16), :] = ro_own[s, r].astype(F32)

    for k in range(1, 8):
        arrived(grad_in.at[k], grad_recv.at[k])
        own_grad = own_grad + grad_in[k].astype(F32)
    cols = pl.ds(pl.multiple_of(group * cols_each, cols_each), cols_each)
    stepped = w[:, cols] - (5.0 / math.sqrt(batch)) * own_grad[:classes]
    trimmed = stepped - jnp.clip(stepped, -1.0, 1.0)
    part = jnp.sum(trimmed * trimmed, axis=0, keepdims=True)
    norm_out[...] = jnp.broadcast_to(part, (8, cols_each))
    for k in range(1, 8):
        b = back[k]
        send(norm_out, norm_in.at[b], norm_send.at[k], norm_recv.at[b], {"frames": frame_dev(k)})
    for k in range(1, 8):
        arrived(norm_in.at[k], norm_recv.at[k])
        part = part + norm_in[k, 0:1, :]
    norm = jnp.sqrt(jnp.sum(part, axis=1, keepdims=True) + 1e-6)
    limit = 1.5 * math.sqrt(w.shape[0] * w.shape[1])
    out_ref[...] = trimmed * jnp.maximum(0.0, 1.0 - limit / norm)

    for copy in sends:
        copy.wait_send()


def body(frames_in, labels, projection, kernel_scale, shift, weights, readout):
    n_feat, n_frames = lax.axis_size("feat"), lax.axis_size("frames")
    rows, depth = frames_in.shape
    classes, columns = weights.shape
    batch = labels.shape[0] * n_frames
    each = columns // n_frames
    vmem = pl.BlockSpec(memory_space=pltpu.VMEM)
    hbm = pl.BlockSpec(memory_space=pl.ANY)
    dma = pltpu.SemaphoreType.DMA
    new_weights, ro_grad = pl.pallas_call(
        functools.partial(kernel, batch, columns * n_feat, classes),
        out_shape=(
            jax.ShapeDtypeStruct((classes, each), F32),
            jax.ShapeDtypeStruct((512, LANES), F32),
        ),
        in_specs=[pl.BlockSpec(memory_space=pltpu.SMEM), hbm, hbm, hbm, vmem, vmem, vmem],
        out_specs=(vmem, vmem),
        scratch_shapes=[
            pltpu.VMEM((rows, depth), BF16),
            pltpu.VMEM((depth, columns), BF16),
            pltpu.VMEM((classes, columns), F32),
            pltpu.VMEM((LANES, columns), BF16),
            pltpu.VMEM((8, 4, rows, depth), BF16),
            pltpu.VMEM((1024, columns), BF16),
            pltpu.VMEM((128, 128), F32),
            pltpu.VMEM((8, 2, rows, LANES), F32),
            pltpu.VMEM((8, 2, rows, LANES), BF16),
            pltpu.VMEM((8, 2, rows, LANES), BF16),
            pltpu.VMEM((8, 2, rows, LANES), BF16),
            pltpu.VMEM((8, 2, rows, LANES), BF16),
            pltpu.VMEM((8, 4, rows, LANES), BF16),
            pltpu.VMEM((ROWS, 1024), BF16),
            pltpu.VMEM((8, ROWS, each), BF16),
            pltpu.VMEM((8, ROWS, each), BF16),
            pltpu.VMEM((512, LANES), F32),
            pltpu.VMEM((16, LANES), BF16),
            pltpu.VMEM((8, 16, LANES), BF16),
            pltpu.VMEM((8, 4, 16, LANES), BF16),
            pltpu.VMEM((8, each), F32),
            pltpu.VMEM((8, 8, each), F32),
            dma((3,)),
            dma((32,)), dma((8, 4)),
            dma((8,)), dma((8,)),
            dma((8, 2)), dma((8, 2)),
            dma((32,)), dma((8, 4)),
            dma((8,)), dma((8,)),
            dma((8,)), dma((8,)),
            dma((32,)), dma((8, 4)),
            dma((8,)), dma((8,)),
        ],
        compiler_params=pltpu.CompilerParams(
            collective_id=0, has_side_effects=True, vmem_limit_bytes=56 * 2**20
        ),
        name="fourier_step",
    )(kernel_scale, frames_in, projection, weights, labels.reshape(8, 128), shift.reshape(1, -1), readout)
    new_readout = readout - 3.0 / math.sqrt(batch) * ro_grad[:depth, :classes].T
    return (new_weights, new_readout)


def solution(mesh):
    return jax.shard_map(
        body,
        mesh=mesh,
        in_specs=(
            P(("frames", "feat"), None),
            P("frames"),
            P(None, "feat"),
            P("feat"),
            P("feat"),
            P(None, "feat"),
            P(),
        ),
        out_specs=(P(None, ("feat", "frames")), P()),
        check_vma=False,
    )
```

time: 689 us -> 101 us (0.15)
  waiting for transfers between devices: 544 us -> 0 us
  Pallas kernels: 0 us -> 95.6 us
  matrix products: 69.6 us -> 0 us
  blocking collectives: 41.6 us -> 0 us
  between operations: 15.2 us -> 1.36 us
  other arithmetic: 11.6 us -> 1.08 us
    psum x3 -> x0, waiting for transfers between devices: 544 us -> none  [the longest x1 244 us: body(): lax.psum(jnp.dot(residual_own, frames_in, preferred_element_type=jnp.floa...]
    pallas_call x0 -> x1, Pallas kernels: none -> 95.6 us  [body(): pl.pallas_call(functools.partial(kernel, batch, columns * n_feat, classes...]
    dot_general x5 -> x0, matrix products: 69.6 us -> none  [the longest x1 59.5 us: body(): jnp.dot(lax.all_gather(frames_in, 'feat', axis=0, tiled=True), projection...]
    all_gather x1 -> x0, blocking collectives: 41.6 us -> none  [body(): lax.all_gather(frames_in, 'feat', axis=0, tiled=True)]
  transfers between devices with their start and end apart: 3 -> 0, of which waited for: 3 -> 0; matrix products, arithmetic and copies ran while one was open for 1% -> 0% of each run, Pallas kernels for 0% -> 0%
where the time goes in v1:
time: 101 us
  Pallas kernels  95.6 us (95%)
  local copies, waits for them, and re-layouts  2.78 us (3%)
  between operations  1.36 us (1%)
  other arithmetic  1.08 us (1%)
    pallas_call x1, Pallas kernels, body(): pl.pallas_call(functools.partial(kernel, batch, columns * n_feat, classes...  95.6 us
    unnamed x5, local copies, waits for them, and re-layouts  2.78 us

profile of v1, /device:TPU:1, one launch (start us, length us, event | category | flops | bytes accessed | tf_op | source)
XLA Modules:
  0.0 100.8 jit_solution(15163302501548579400)
XLA Ops:
  0.6 0.0 copy-start
  1.3 95.6 %fourier_step.1 = (f32[147,512]{1,0:T(8,128)}, f32[512,256]{1,0:T(8,128)}) custom-call(f32[1]{0:T(128)S(6)} %copy.12.scale_ref, bf16[32,440]{1,0:T(8,128)(2,1)} %x_hbm.1, bf16[440,4096]{1,0:T(8,128)(2,1)} %proj_hbm.1, f32[147,4096]{1,0:T(8,128)} %w_hbm.1, s32[8,128]{1,0:T(8,128)} %bitcast.5, f32[1,4096]{1,0:T(1,128)} %bitcast.4, f32[147,440]{1,0:T(8,128)} %readout_ref.1), custom_call_target="tpu_custom_call" | custom-call | tf_op jit(solution)/shard_map/fourier_step/pallas_call | solution.py:283
  96.9 0.0 copy-done
  96.9 0.2 copy.9
  97.1 1.1 %bitcast_subtract_fusion = f32[147,440]{0,1:T(8,128)S(1)} fusion(f32[147,440]{0,1:T(8,128)S(1)} %copy.9, f32[512,256]{1,0:T(8,128)} %get-tuple-element.5), kind=kLoop, calls=%fused_computation | loop fusion | flops 129360 | bytes 776160 | tf_op jit(solution)/shard_map/sub | solution.py:329
  98.2 0.9 copy.10
  99.1 1.7 %copy.13 = f32[147,512]{1,0:T(8,128)} copy(f32[147,512]{1,0:T(8,128)} %get-tuple-element.10) | data formatting | bytes 602112
Async XLA Ops:
  0.6 96.3 %copy-start = (f32[147,440]{1,0:T(8,128)S(1)}, f32[147,440]{1,0:T(8,128)}, u32[]{:S(2)}) copy-start(f32[147,440]{1,0:T(8,128)} %readout_ref.1) | copy-start | bytes 776164

commit v2 on v1

v2 whole, which is shorter than its diff:
```python
import functools
import math

import jax
import jax.numpy as jnp
from jax import lax
from jax.experimental import pallas as pl
from jax.experimental.pallas import tpu as pltpu
from jax.sharding import PartitionSpec as P

MESH = pl.DeviceIdType.MESH
F32, BF16 = jnp.float32, jnp.bfloat16
ROWS = 160
NB = 256

OFFS = (0, 1, -1, 2, -2, 3, -3, 4)
MIRROR = tuple(OFFS.index(-d) if -d in OFFS else OFFS.index(d) for d in OFFS)
CHUNKS = ((0, 1), (1, 3), (3, 5), (5, 7), (7, 8))

COS = (1.4142124652862549, -27.91513442993164, 91.82299041748047, -120.59228515625, 83.1423110961914, -29.799043655395508)


def features_of(product, scale, shift):
    turns = product * scale + shift
    r = turns - jnp.round(turns)
    u = r * r
    acc = COS[-1] * u + COS[-2]
    for c in COS[-3::-1]:
        acc = acc * u + c
    return acc.astype(BF16)


def kernel(
    batch, feat_total, classes,
    scale_ref, x_hbm, proj_hbm, w_hbm, labels_hbm, shift_hbm, readout_hbm,
    out_ref, factor_ref, readout_out_ref,
    x_own, proj, w, labels, shift, readout, w_low, x_all, feats, sum_out, sum_in, loc, res_all, res_t,
    grad_out, grad_in, ro_pad, ro_out, ro_in, ro_all, norm_out, norm_in,
    local_sem, x_send, x_recv, sum_send, sum_recv, loc_send, loc_recv, res_send, res_recv, res_pass, res_got,
    grad_send, grad_recv, ro_send, ro_recv, all_send, all_recv, norm_send, norm_recv,
):
    me = lax.axis_index("feat")
    group = lax.axis_index("frames")
    z, q = me // 4, me % 4
    xh, y = group // 4, group % 4
    core = q % 2
    q_sib = q + 1 - 2 * core
    q_x = (q + 2) % 4

    def feat_dev(d, qq):
        return {"feat": ((z + d + 8) % 8) * 4 + qq}

    def frame_dev(k):
        dx, dy = k // 4, k % 4
        return ((xh + dx) % 2) * 4 + (y + dy) % 4

    sibling, neighbour, across = feat_dev(0, q_sib), feat_dev(0, q_x), feat_dev(0, 3 - q)
    sends = []

    def send(src, dst, ssem, rsem, dev):
        copy = pltpu.make_async_remote_copy(
            src_ref=src, dst_ref=dst, send_sem=ssem, recv_sem=rsem, device_id=dev, device_id_type=MESH
        )
        copy.start()
        sends.append(copy)

    def arrived(ref, rsem):
        pltpu.make_async_remote_copy(
            src_ref=ref, dst_ref=ref, send_sem=x_send.at[0], recv_sem=rsem, device_id=sibling, device_id_type=MESH
        ).wait_recv()

    local = [
        pltpu.make_async_copy(src, dst, local_sem.at[i])
        for i, (src, dst) in enumerate(
            ((x_hbm, x_own), (shift_hbm, shift), (proj_hbm, proj), (w_hbm, w), (labels_hbm, labels), (readout_hbm, readout))
        )
    ]
    for copy in local:
        copy.start()

    barrier = pltpu.get_barrier_semaphore()
    partners = [feat_dev(d, q) for d in OFFS[1:]] + [neighbour, across, sibling]
    partners += [{"frames": frame_dev(k)} for k in range(1, 8)]
    for dev in partners:
        pl.semaphore_signal(barrier, inc=1, device_id=dev, device_id_type=MESH)
    local[0].wait()
    x_all[0, q] = x_own[...]
    pl.semaphore_wait(barrier, len(partners))

    def gather_start(buf, ss, rs, at, at_mirror):
        gather_local(buf, ss, rs, at, 0, False)
        for s in range(1, 8):
            m = MIRROR[s]
            send(buf.at[at(0), q], buf.at[at_mirror(m), q], ss.at[s], rs.at[m, 0], feat_dev(OFFS[s], q))

    def gather_local(buf, ss, rs, at, s, wait=True):
        piece = buf.at[at(s), q]
        if wait:
            arrived(piece, rs.at[s, 0])
        send(piece, piece, ss.at[8 + s], rs.at[s, 2], neighbour)
        send(piece, piece, ss.at[16 + s], rs.at[s, 1], sibling)

    def gather_last(buf, ss, rs, at, s):
        piece = buf.at[at(s), q_x]
        arrived(piece, rs.at[s, 2])
        send(piece, piece, ss.at[24 + s], rs.at[s, 3], sibling)

    def gather_wait(buf, rs, at, s):
        arrived(buf.at[at(s), q_sib], rs.at[s, 1])
        arrived(buf.at[at(s), 3 - q], rs.at[s, 3])

    def relative(s):
        return s

    def x_local(*slots):
        for s in slots:
            gather_local(x_all, x_send, x_recv, relative, s)

    def x_last(*slots):
        for s in slots:
            gather_last(x_all, x_send, x_recv, relative, s)

    def x_wait(*slots):
        for s in slots:
            gather_wait(x_all, x_recv, relative, s)

    gather_start(x_all, x_send, x_recv, relative, relative)

    w_low[144:ROWS, :] = jnp.zeros((ROWS - 144, w_low.shape[1]), BF16)
    local[3].wait()
    w_low[0:classes, :] = w[...].astype(BF16)
    local[1].wait()
    local[2].wait()

    nt = (((1,), (1,)), ((), ()))
    turn = 1.0 / (2.0 * math.pi)
    scale = scale_ref[0] * turn

    def half(chunk, first):
        lo, hi = CHUNKS[chunk]
        n = (hi - lo) * 128
        xs = x_all[lo:hi].reshape(n, x_all.shape[-1])

        def block(j, carry):
            cols = pl.ds(pl.multiple_of(j * NB, NB), NB)
            product = jnp.dot(xs, proj[:, cols], preferred_element_type=F32)
            feats[lo * 128 : hi * 128, cols] = features_of(product, scale, shift[:, cols] * turn)
            return carry

        count = feats.shape[1] // NB // 2
        lax.fori_loop(first * count, (first + 1) * count, block, 0, unroll=True)

    def scores(chunk):
        lo, hi = CHUNKS[chunk]
        part = lax.dot_general(w_low[...], feats[lo * 128 : hi * 128, :], nt, preferred_element_type=F32)
        for s in range(lo, hi):
            if s == 0:
                return part
            m = MIRROR[s]
            sum_out[s] = part[:, (s - lo) * 128 : (s - lo + 1) * 128].astype(BF16)
            send(sum_out.at[s], sum_in.at[m], sum_send.at[s], sum_recv.at[m], feat_dev(OFFS[s], q))

    x_last(0)
    x_local(1, 2)
    x_wait(0)
    half(0, 0)
    x_local(3, 4)
    x_last(1, 2)
    half(0, 1)
    total = scores(0)
    x_wait(1, 2)
    half(1, 0)
    x_local(5, 6)
    x_last(3, 4)
    half(1, 1)
    scores(1)
    x_wait(3, 4)
    x_local(7)
    half(2, 0)
    x_last(5, 6)
    half(2, 1)
    scores(2)
    x_wait(5, 6)
    half(3, 0)
    x_last(7)
    half(3, 1)
    scores(3)
    x_wait(7)
    half(4, 0)
    half(4, 1)
    scores(4)

    local[4].wait()
    local[5].wait()
    ro = readout[...]
    ro_hi = ro.astype(BF16)
    rest = ro - ro_hi.astype(F32)
    ro_mid = rest.astype(BF16)
    ro_lo = (rest - ro_mid.astype(F32)).astype(BF16)
    x0 = x_all[0].reshape(128, x_all.shape[-1])
    linear = (
        lax.dot_general(ro_hi, x0, nt, preferred_element_type=F32)
        + lax.dot_general(ro_mid, x0, nt, preferred_element_type=F32)
        + lax.dot_general(ro_lo, x0, nt, preferred_element_type=F32)
    )
    linear = jnp.concatenate([linear, jnp.zeros((ROWS - classes, 128), F32)], axis=0)

    for s in range(1, 8):
        arrived(sum_in.at[s], sum_recv.at[s])
        total = total + sum_in[s].astype(F32)
    loc[q] = total.astype(BF16)
    mine = loc.at[q]
    send(mine, mine, loc_send.at[2], loc_recv.at[2], neighbour)
    send(mine, mine, loc_send.at[3], loc_recv.at[3], across)
    send(mine, mine, loc_send.at[1], loc_recv.at[1], sibling)
    arrived(loc.at[q_sib], loc_recv.at[1])
    arrived(loc.at[q_x], loc_recv.at[2])
    arrived(loc.at[3 - q], loc_recv.at[3])
    total = loc[0].astype(F32)
    for k in range(1, 4):
        total = total + loc[k].astype(F32)
    rows = lax.broadcasted_iota(jnp.int32, (ROWS, 128), 0)
    inside = rows < classes
    value = jnp.where(inside, total * (1.0 / math.sqrt(feat_total)) + linear, -1e30)
    value = jnp.exp(value - jnp.max(value, axis=0, keepdims=True))
    probs = value / jnp.sum(value, axis=0, keepdims=True)
    label = labels[pl.ds(z, 1), :]
    residual = jnp.where(rows == label, probs - 1.0, probs)
    res_all[0] = residual.astype(BF16).reshape(2, ROWS // 2, 128)

    for s in range(1, 8):
        m = MIRROR[s]
        send(res_all.at[0, core], res_all.at[m, core], res_send.at[s], res_recv.at[m], feat_dev(OFFS[s], q))
    for s in range(1, 8):
        piece = res_all.at[s, core]
        arrived(piece, res_recv.at[s])
        send(piece, piece, res_pass.at[s], res_got.at[s], sibling)
    for s in range(8):
        if s:
            arrived(res_all.at[s, 1 - core], res_got.at[s])
        res_t[:, s * 128 : (s + 1) * 128] = res_all[s].reshape(ROWS, 128)

    cols_each = out_ref.shape[1]

    def grad_block(k):
        cols = pl.ds(pl.multiple_of(frame_dev(k) * cols_each, cols_each), cols_each)
        return jnp.dot(res_t[...], feats[:, cols], preferred_element_type=F32)

    back = [0] + [(k // 4) * 4 + (4 - k % 4) % 4 for k in range(1, 8)]

    def grad_send_block(k):
        grad_out[k] = grad_block(k).astype(BF16)
        b = back[k]
        send(grad_out.at[k], grad_in.at[b], grad_send.at[k], grad_recv.at[b], {"frames": frame_dev(k)})

    grad_send_block(6)

    ro_pad[...] = jnp.zeros_like(ro_pad)
    depth = x_all.shape[-1]
    ro_pad[0:ROWS, 0:depth] = jnp.dot(res_t[...], x_all[...].reshape(1024, depth), preferred_element_type=F32)
    ro_mine = ro_pad[pl.ds(pl.multiple_of(z * 32, 32), 32), pl.ds(pl.multiple_of(q * 128, 128), 128)]
    ro_out[...] = ro_mine.astype(BF16)
    for k in range(1, 8):
        b = back[k]
        send(ro_out, ro_in.at[b], ro_send.at[k], ro_recv.at[b], {"frames": frame_dev(k)})

    for k in (5, 7, 2, 4, 1, 3):
        grad_send_block(k)
    own_grad = grad_block(0)

    def absolute(s):
        return (z + OFFS[s] + 8) % 8

    def mine_at(m):
        return z

    for k in range(1, 8):
        arrived(ro_in.at[k], ro_recv.at[k])
        ro_mine = ro_mine + ro_in[k].astype(F32)
    ro_all[z, q] = ro_mine.astype(BF16)
    gather_start(ro_all, all_send, all_recv, absolute, mine_at)
    gather_last(ro_all, all_send, all_recv, absolute, 0)
    for s in range(1, 8):
        gather_local(ro_all, all_send, all_recv, absolute, s)
    for s in range(1, 8):
        gather_last(ro_all, all_send, all_recv, absolute, s)
    for s in range(8):
        gather_wait(ro_all, all_recv, absolute, s)
    for i in range(0, classes, 32):
        n = min(32, classes - i)
        grad = jnp.concatenate([ro_all[i // 32, k] for k in range(4)], axis=1).astype(F32)
        readout_out_ref[i : i + n, :] = ro[i : i + n] - (3.0 / math.sqrt(batch)) * grad[:n, :depth]

    for k in (3, 1, 4, 2, 7, 5, 6):
        arrived(grad_in.at[k], grad_recv.at[k])
        own_grad = own_grad + grad_in[k].astype(F32)
    cols = pl.ds(pl.multiple_of(group * cols_each, cols_each), cols_each)
    stepped = w[:, cols] - (5.0 / math.sqrt(batch)) * own_grad[:classes]
    trimmed = stepped - jnp.clip(stepped, -1.0, 1.0)
    part = jnp.sum(trimmed * trimmed, axis=0, keepdims=True)
    part = part[:, 0:128] + part[:, 128:256] + part[:, 256:384] + part[:, 384:512]
    norm_out[...] = jnp.broadcast_to(part, (8, 128))
    for k in range(1, 8):
        b = back[k]
        send(norm_out, norm_in.at[b], norm_send.at[k], norm_recv.at[b], {"frames": frame_dev(k)})
    out_ref[...] = trimmed
    for k in range(1, 8):
        arrived(norm_in.at[k], norm_recv.at[k])
        part = part + norm_in[k, 0:1, :]
    norm = jnp.sqrt(jnp.sum(part, axis=1, keepdims=True) + 1e-6)
    limit = 1.5 * math.sqrt(w.shape[0] * w.shape[1])
    factor_ref[...] = jnp.broadcast_to(jnp.maximum(0.0, 1.0 - limit / norm), (8, 128))

    for copy in sends:
        copy.wait_send()


def body(frames_in, labels, projection, kernel_scale, shift, weights, readout):
    n_feat, n_frames = lax.axis_size("feat"), lax.axis_size("frames")
    rows, depth = frames_in.shape
    classes, columns = weights.shape
    batch = labels.shape[0] * n_frames
    each = columns // n_frames
    vmem = pl.BlockSpec(memory_space=pltpu.VMEM)
    hbm = pl.BlockSpec(memory_space=pl.ANY)
    dma = pltpu.SemaphoreType.DMA
    trimmed, factor, new_readout = pl.pallas_call(
        functools.partial(kernel, batch, columns * n_feat, classes),
        out_shape=(
            jax.ShapeDtypeStruct((classes, each), F32),
            jax.ShapeDtypeStruct((8, 128), F32),
            jax.ShapeDtypeStruct(readout.shape, F32),
        ),
        in_specs=[pl.BlockSpec(memory_space=pltpu.SMEM)] + [hbm] * 6,
        out_specs=(vmem, vmem, vmem),
        scratch_shapes=[
            pltpu.VMEM((rows, depth), BF16),
            pltpu.VMEM((depth, columns), BF16),
            pltpu.VMEM((classes, columns), F32),
            pltpu.VMEM((8, 128), jnp.int32),
            pltpu.VMEM((1, columns), F32),
            pltpu.VMEM(readout.shape, F32),
            pltpu.VMEM((ROWS, columns), BF16),
            pltpu.VMEM((8, 4, rows, depth), BF16),
            pltpu.VMEM((1024, columns), BF16),
            pltpu.VMEM((8, ROWS, 128), BF16),
            pltpu.VMEM((8, ROWS, 128), BF16),
            pltpu.VMEM((4, ROWS, 128), BF16),
            pltpu.VMEM((8, 2, ROWS // 2, 128), BF16),
            pltpu.VMEM((ROWS, 1024), BF16),
            pltpu.VMEM((8, ROWS, each), BF16),
            pltpu.VMEM((8, ROWS, each), BF16),
            pltpu.VMEM((256, 512), F32),
            pltpu.VMEM((32, 128), BF16),
            pltpu.VMEM((8, 32, 128), BF16),
            pltpu.VMEM((8, 4, 32, 128), BF16),
            pltpu.VMEM((8, 128), F32),
            pltpu.VMEM((8, 8, 128), F32),
            dma((6,)),
            dma((32,)), dma((8, 4)),
            dma((8,)), dma((8,)),
            dma((4,)), dma((4,)),
            dma((8,)), dma((8,)), dma((8,)), dma((8,)),
            dma((8,)), dma((8,)),
            dma((8,)), dma((8,)),
            dma((32,)), dma((8, 4)),
            dma((8,)), dma((8,)),
        ],
        compiler_params=pltpu.CompilerParams(
            collective_id=0, has_side_effects=True, vmem_limit_bytes=56 * 2**20
        ),
        name="fourier_step",
    )(kernel_scale, frames_in, projection, weights, labels.reshape(8, 128), shift.reshape(1, -1), readout)
    return (trimmed * factor[0, 0], new_readout)


def solution(mesh):
    return jax.shard_map(
        body,
        mesh=mesh,
        in_specs=(
            P(("frames", "feat"), None),
            P("frames"),
            P(None, "feat"),
            P("feat"),
            P("feat"),
            P(None, "feat"),
            P(),
        ),
        out_specs=(P(None, ("feat", "frames")), P()),
        check_vma=False,
    )
```

time: 101 us -> 86.1 us (0.85)
  Pallas kernels: 95.6 us -> 79.4 us
  other arithmetic: 1.08 us -> 2.35 us
    pallas_call x1, Pallas kernels: 95.6 us -> 79.4 us  [body(): pl.pallas_call(functools.partial(kernel, batch, columns * n_feat, classes...]
    mul x0 -> x1, other arithmetic: none -> 2.35 us  [body(): return (trimmed * factor[0, 0], new_readout)]
    slice x0 -> x1, local copies, waits for them, and re-layouts: none -> 1.19 us  [body(): return (trimmed * factor[0, 0], new_readout)]
    sub x1 -> x0, other arithmetic: 1.08 us -> none  [body(): new_readout = readout - 3.0 / math.sqrt(batch) * ro_grad[:depth, :classes].T]
    unnamed x5 -> x1, local copies, waits for them, and re-layouts: 2.78 us -> 1.71 us
where the time goes in v2:
time: 86.1 us; the launch traced here: 85.9 us
  Pallas kernels  79.4 us (92%)
  local copies, waits for them, and re-layouts  2.89 us (3%)
  other arithmetic  2.35 us (3%)
  between operations  1.29 us (1%)
    pallas_call x1, Pallas kernels, body(): pl.pallas_call(functools.partial(kernel, batch, columns * n_feat, classes...  79.4 us
    mul x1, other arithmetic, body(): return (trimmed * factor[0, 0], new_readout)  2.35 us

profile of v2, /device:TPU:1, one launch (start us, length us, event | category | flops | bytes accessed | tf_op | source)
XLA Modules:
  0.0 85.9 jit_solution(76166258759009989)
XLA Ops:
  1.3 79.4 %fourier_step.1 = (f32[147,512]{1,0:T(8,128)}, f32[8,128]{1,0:T(8,128)}, f32[147,440]{1,0:T(8,128)}) custom-call(f32[1]{0:T(128)S(6)} %copy.10.scale_ref, bf16[32,440]{1,0:T(8,128)(2,1)} %x_hbm.1, bf16[440,4096]{1,0:T(8,128)(2,1)} %proj_hbm.1, f32[147,4096]{1,0:T(8,128)} %w_hbm.1, s32[8,128]{1,0:T(8,128)} %bitcast.4, f32[1,4096]{1,0:T(1,128)} %bitcast.3, ...), custom_call_target="tpu_custom_call" | custom-call | tf_op jit(solution)/shard_map/fourier_step/pallas_call | solution.py:327
  80.6 1.2 %slice.3 = f32[1,1]{1,0:T(1,128)} slice(f32[8,128]{1,0:T(8,128)} %get-tuple-element.6), slice={[0:1], [0:1]} | slice | bytes 8 | tf_op jit(solution)/shard_map/slice | solution.py:374
  81.8 2.4 %broadcast_multiply_fusion = f32[147,512]{1,0:T(8,128)} fusion(f32[147,512]{1,0:T(8,128)} %get-tuple-element.5, f32[]{:T(128)} %bitcast.2), kind=kLoop, calls=%fused_computation | loop fusion | flops 75264 | bytes 602116 | tf_op jit(solution)/shard_map/mul | solution.py:374
  84.2 1.7 %copy.11 = f32[147,440]{1,0:T(8,128)} copy(f32[147,440]{1,0:T(8,128)} %get-tuple-element.11) | data formatting | bytes 517440

commit v3 on v2

--- a/solution.py
+++ b/solution.py
@@ -33,11 +33,11 @@
 def kernel(
     batch, feat_total, classes,
     scale_ref, x_hbm, proj_hbm, w_hbm, labels_hbm, shift_hbm, readout_hbm,
-    out_ref, factor_ref, readout_out_ref,
+    out_ref, readout_out_ref,
     x_own, proj, w, labels, shift, readout, w_low, x_all, feats, sum_out, sum_in, loc, res_all, res_t,
     grad_out, grad_in, ro_pad, ro_out, ro_in, ro_all, norm_out, norm_in,
     local_sem, x_send, x_recv, sum_send, sum_recv, loc_send, loc_recv, res_send, res_recv, res_pass, res_got,
-    grad_send, grad_recv, ro_send, ro_recv, all_send, all_recv, norm_send, norm_recv,
+    grad_send, grad_recv, ro_send, ro_recv, all_send, all_recv, all_pass, all_got, norm_send, norm_recv,
 ):
     me = lax.axis_index("feat")
     group = lax.axis_index("frames")
@@ -168,21 +168,21 @@
     x_last(1, 2)
     half(0, 1)
     total = scores(0)
+    x_local(5, 6)
+    x_last(3, 4)
     x_wait(1, 2)
     half(1, 0)
-    x_local(5, 6)
-    x_last(3, 4)
+    x_local(7)
     half(1, 1)
     scores(1)
+    x_last(5, 6)
     x_wait(3, 4)
-    x_local(7)
     half(2, 0)
-    x_last(5, 6)
+    x_last(7)
     half(2, 1)
     scores(2)
     x_wait(5, 6)
     half(3, 0)
-    x_last(7)
     half(3, 1)
     scores(3)
     x_wait(7)
@@ -258,7 +258,7 @@
     ro_pad[...] = jnp.zeros_like(ro_pad)
     depth = x_all.shape[-1]
     ro_pad[0:ROWS, 0:depth] = jnp.dot(res_t[...], x_all[...].reshape(1024, depth), preferred_element_type=F32)
-    ro_mine = ro_pad[pl.ds(pl.multiple_of(z * 32, 32), 32), pl.ds(pl.multiple_of(q * 128, 128), 128)]
+    ro_mine = ro_pad[pl.ds(pl.multiple_of(z * 32, 32), 32), pl.ds(pl.multiple_of(core * 256, 256), 256)]
     ro_out[...] = ro_mine.astype(BF16)
     for k in range(1, 8):
         b = back[k]
@@ -268,28 +268,18 @@
         grad_send_block(k)
     own_grad = grad_block(0)
 
-    def absolute(s):
-        return (z + OFFS[s] + 8) % 8
-
-    def mine_at(m):
-        return z
-
     for k in range(1, 8):
         arrived(ro_in.at[k], ro_recv.at[k])
         ro_mine = ro_mine + ro_in[k].astype(F32)
-    ro_all[z, q] = ro_mine.astype(BF16)
-    gather_start(ro_all, all_send, all_recv, absolute, mine_at)
-    gather_last(ro_all, all_send, all_recv, absolute, 0)
-    for s in range(1, 8):
-        gather_local(ro_all, all_send, all_recv, absolute, s)
-    for s in range(1, 8):
-        gather_last(ro_all, all_send, all_recv, absolute, s)
-    for s in range(8):
-        gather_wait(ro_all, all_recv, absolute, s)
-    for i in range(0, classes, 32):
-        n = min(32, classes - i)
-        grad = jnp.concatenate([ro_all[i // 32, k] for k in range(4)], axis=1).astype(F32)
-        readout_out_ref[i : i + n, :] = ro[i : i + n] - (3.0 / math.sqrt(batch)) * grad[:n, :depth]
+    ro_all[z, core] = ro_mine.astype(BF16)
+    mine = ro_all.at[z, core]
+    for s in range(1, 8):
+        send(mine, mine, all_send.at[s], all_recv.at[MIRROR[s]], feat_dev(OFFS[s], q))
+    send(mine, mine, all_pass.at[0], all_got.at[0], sibling)
+    for s in range(1, 8):
+        piece = ro_all.at[(z + OFFS[s] + 8) % 8, core]
+        arrived(piece, all_recv.at[s])
+        send(piece, piece, all_pass.at[s], all_got.at[s], sibling)
 
     for k in (3, 1, 4, 2, 7, 5, 6):
         arrived(grad_in.at[k], grad_recv.at[k])
@@ -303,13 +293,18 @@
     for k in range(1, 8):
         b = back[k]
         send(norm_out, norm_in.at[b], norm_send.at[k], norm_recv.at[b], {"frames": frame_dev(k)})
-    out_ref[...] = trimmed
+    for s in range(8):
+        arrived(ro_all.at[(z + OFFS[s] + 8) % 8, 1 - core], all_got.at[s])
+    for i in range(0, classes, 32):
+        n = min(32, classes - i)
+        grad = jnp.concatenate([ro_all[i // 32, k] for k in range(2)], axis=1).astype(F32)
+        readout_out_ref[i : i + n, :] = ro[i : i + n] - (3.0 / math.sqrt(batch)) * grad[:n, :depth]
     for k in range(1, 8):
         arrived(norm_in.at[k], norm_recv.at[k])
         part = part + norm_in[k, 0:1, :]
     norm = jnp.sqrt(jnp.sum(part, axis=1, keepdims=True) + 1e-6)
     limit = 1.5 * math.sqrt(w.shape[0] * w.shape[1])
-    factor_ref[...] = jnp.broadcast_to(jnp.maximum(0.0, 1.0 - limit / norm), (8, 128))
+    out_ref[...] = trimmed * jnp.maximum(0.0, 1.0 - limit / norm)
 
     for copy in sends:
         copy.wait_send()
@@ -324,15 +319,14 @@
     vmem = pl.BlockSpec(memory_space=pltpu.VMEM)
     hbm = pl.BlockSpec(memory_space=pl.ANY)
     dma = pltpu.SemaphoreType.DMA
-    trimmed, factor, new_readout = pl.pallas_call(
+    return pl.pallas_call(
         functools.partial(kernel, batch, columns * n_feat, classes),
         out_shape=(
-            jax.ShapeDtypeStruct((classes, each), F32),
-            jax.ShapeDtypeStruct((8, 128), F32),
-            jax.ShapeDtypeStruct(readout.shape, F32),
+            pltpu.VMEM((classes, each), F32),
+            pltpu.VMEM(readout.shape, F32),
         ),
         in_specs=[pl.BlockSpec(memory_space=pltpu.SMEM)] + [hbm] * 6,
-        out_specs=(vmem, vmem, vmem),
+        out_specs=(vmem, vmem),
         scratch_shapes=[
             pltpu.VMEM((rows, depth), BF16),
             pltpu.VMEM((depth, columns), BF16),
@@ -351,9 +345,9 @@
             pltpu.VMEM((8, ROWS, each), BF16),
             pltpu.VMEM((8, ROWS, each), BF16),
             pltpu.VMEM((256, 512), F32),
-            pltpu.VMEM((32, 128), BF16),
-            pltpu.VMEM((8, 32, 128), BF16),
-            pltpu.VMEM((8, 4, 32, 128), BF16),
+            pltpu.VMEM((32, 256), BF16),
+            pltpu.VMEM((8, 32, 256), BF16),
+            pltpu.VMEM((8, 2, 32, 256), BF16),
             pltpu.VMEM((8, 128), F32),
             pltpu.VMEM((8, 8, 128), F32),
             dma((6,)),
@@ -363,7 +357,7 @@
             dma((8,)), dma((8,)), dma((8,)), dma((8,)),
             dma((8,)), dma((8,)),
             dma((8,)), dma((8,)),
-            dma((32,)), dma((8, 4)),
+            dma((8,)), dma((8,)), dma((8,)), dma((8,)),
             dma((8,)), dma((8,)),
         ],
         compiler_params=pltpu.CompilerParams(
@@ -371,7 +365,6 @@
         ),
         name="fourier_step",
     )(kernel_scale, frames_in, projection, weights, labels.reshape(8, 128), shift.reshape(1, -1), readout)
-    return (trimmed * factor[0, 0], new_readout)
 
 
 def solution(mesh):

time: 86.1 us -> 77.5 us (0.900)
  Pallas kernels: 79.4 us -> 73.7 us
  other arithmetic: 2.35 us -> 0 us
  local copies, waits for them, and re-layouts: 2.89 us -> 1.44 us
    pallas_call x1, Pallas kernels: 79.4 us -> 73.7 us  [body(): pl.pallas_call(functools.partial(kernel, batch, columns * n_feat, classes...]
    mul x1 -> x0, other arithmetic: 2.35 us -> none  [body(): return (trimmed * factor[0, 0], new_readout)]
    slice x1 -> x0, local copies, waits for them, and re-layouts: 1.19 us -> none  [body(): return (trimmed * factor[0, 0], new_readout)]
where the time goes in v3:
time: 77.5 us; the launch traced here: 76.5 us
  Pallas kernels  73.7 us (95%)
  local copies, waits for them, and re-layouts  1.44 us (2%)
  between operations  1.29 us (2%)
    pallas_call x1, Pallas kernels, body(): pl.pallas_call(functools.partial(kernel, batch, columns * n_feat, classes...  73.7 us

profile of v3, /device:TPU:1, one launch (start us, length us, event | category | flops | bytes accessed | tf_op | source)
XLA Modules:
  0.0 76.5 jit_solution(13300767088174898686)
XLA Ops:
  1.3 73.7 %fourier_step.1 = (f32[147,512]{1,0:T(8,128)S(1)}, f32[147,440]{1,0:T(8,128)S(1)}) custom-call(f32[1]{0:T(128)S(6)} %copy.13.scale_ref, bf16[32,440]{1,0:T(8,128)(2,1)} %x_hbm.1, bf16[440,4096]{1,0:T(8,128)(2,1)} %proj_hbm.1, f32[147,4096]{1,0:T(8,128)} %w_hbm.1, s32[8,128]{1,0:T(8,128)} %bitcast.3, f32[1,4096]{1,0:T(1,128)} %bitcast.2, f32[147,440]{1,0:T(8,128)} %readout_hbm.1), custom_call_target="tpu_custom_call" | custom-call | tf_op jit(solution)/shard_map/fourier_step/pallas_call | solution.py:322
  75.0 0.7 copy.11
  75.7 0.7 copy.12

commit v4 on v3

--- a/solution.py
+++ b/solution.py
@@ -12,6 +12,7 @@
 F32, BF16 = jnp.float32, jnp.bfloat16
 ROWS = 160
 NB = 256
+XF = 256
 
 OFFS = (0, 1, -1, 2, -2, 3, -3, 4)
 MIRROR = tuple(OFFS.index(-d) if -d in OFFS else OFFS.index(d) for d in OFFS)
@@ -34,10 +35,10 @@
     batch, feat_total, classes,
     scale_ref, x_hbm, proj_hbm, w_hbm, labels_hbm, shift_hbm, readout_hbm,
     out_ref, readout_out_ref,
-    x_own, proj, w, labels, shift, readout, w_low, x_all, feats, sum_out, sum_in, loc, res_all, res_t,
-    grad_out, grad_in, ro_pad, ro_out, ro_in, ro_all, norm_out, norm_in,
-    local_sem, x_send, x_recv, sum_send, sum_recv, loc_send, loc_recv, res_send, res_recv, res_pass, res_got,
-    grad_send, grad_recv, ro_send, ro_recv, all_send, all_recv, all_pass, all_got, norm_send, norm_recv,
+    proj, w, labels, shift, readout, w_low, x_all, feats, kept, pair_out, pair_in, sum_out, sum_in, loc, final, res_all, res_t,
+    gx_out, gx_in, gy_out, gy_in, cy_out, cy_in, cx, kx, ky, ro_pad, ro_out, ro_in, ro_all, norm_out, norm_in,
+    local_sem, x_send, x_recv, pair_send, pair_recv, sum_send, sum_recv, loc_send, loc_recv, res_send, res_recv, res_pass, res_got,
+    gx_send, gx_recv, gy_send, gy_recv, cy_send, cy_recv, cx_send, cx_recv, ro_send, ro_recv, all_send, all_recv, all_pass, all_got, norm_send, norm_recv,
 ):
     me = lax.axis_index("feat")
     group = lax.axis_index("frames")
@@ -72,7 +73,7 @@
     local = [
         pltpu.make_async_copy(src, dst, local_sem.at[i])
         for i, (src, dst) in enumerate(
-            ((x_hbm, x_own), (shift_hbm, shift), (proj_hbm, proj), (w_hbm, w), (labels_hbm, labels), (readout_hbm, readout))
+            ((x_hbm, x_all.at[0, q]), (shift_hbm, shift), (proj_hbm, proj), (w_hbm, w), (labels_hbm, labels), (readout_hbm, readout))
         )
     ]
     for copy in local:
@@ -83,54 +84,41 @@
     partners += [{"frames": frame_dev(k)} for k in range(1, 8)]
     for dev in partners:
         pl.semaphore_signal(barrier, inc=1, device_id=dev, device_id_type=MESH)
-    local[0].wait()
-    x_all[0, q] = x_own[...]
     pl.semaphore_wait(barrier, len(partners))
 
-    def gather_start(buf, ss, rs, at, at_mirror):
-        gather_local(buf, ss, rs, at, 0, False)
-        for s in range(1, 8):
-            m = MIRROR[s]
-            send(buf.at[at(0), q], buf.at[at_mirror(m), q], ss.at[s], rs.at[m, 0], feat_dev(OFFS[s], q))
-
-    def gather_local(buf, ss, rs, at, s, wait=True):
-        piece = buf.at[at(s), q]
-        if wait:
-            arrived(piece, rs.at[s, 0])
-        send(piece, piece, ss.at[8 + s], rs.at[s, 2], neighbour)
-        send(piece, piece, ss.at[16 + s], rs.at[s, 1], sibling)
-
-    def gather_last(buf, ss, rs, at, s):
-        piece = buf.at[at(s), q_x]
-        arrived(piece, rs.at[s, 2])
-        send(piece, piece, ss.at[24 + s], rs.at[s, 3], sibling)
-
-    def gather_wait(buf, rs, at, s):
-        arrived(buf.at[at(s), q_sib], rs.at[s, 1])
-        arrived(buf.at[at(s), 3 - q], rs.at[s, 3])
-
-    def relative(s):
-        return s
+    def gather_local(s):
+        piece = x_all.at[s, q]
+        source = piece if s else x_hbm
+        if s:
+            arrived(piece, x_recv.at[s, 0])
+        send(source, piece, x_send.at[8 + s], x_recv.at[s, 2], neighbour)
+        send(source, piece, x_send.at[24 + s], x_recv.at[s, 3], across)
+        send(source, piece, x_send.at[16 + s], x_recv.at[s, 1], sibling)
+
+    def gather_wait(s):
+        arrived(x_all.at[s, q_sib], x_recv.at[s, 1])
+        arrived(x_all.at[s, q_x], x_recv.at[s, 2])
+        arrived(x_all.at[s, 3 - q], x_recv.at[s, 3])
 
     def x_local(*slots):
         for s in slots:
-            gather_local(x_all, x_send, x_recv, relative, s)
-
-    def x_last(*slots):
-        for s in slots:
-            gather_last(x_all, x_send, x_recv, relative, s)
+            gather_local(s)
 
     def x_wait(*slots):
         for s in slots:
-            gather_wait(x_all, x_recv, relative, s)
-
-    gather_start(x_all, x_send, x_recv, relative, relative)
+            gather_wait(s)
+
+    gather_local(0)
+    for s in range(1, 8):
+        m = MIRROR[s]
+        send(x_hbm, x_all.at[m, q], x_send.at[s], x_recv.at[m, 0], feat_dev(OFFS[s], q))
 
     w_low[144:ROWS, :] = jnp.zeros((ROWS - 144, w_low.shape[1]), BF16)
     local[3].wait()
     w_low[0:classes, :] = w[...].astype(BF16)
     local[1].wait()
     local[2].wait()
+    local[0].wait()
 
     nt = (((1,), (1,)), ((), ()))
     turn = 1.0 / (2.0 * math.pi)
@@ -154,39 +142,46 @@
         lo, hi = CHUNKS[chunk]
         part = lax.dot_general(w_low[...], feats[lo * 128 : hi * 128, :], nt, preferred_element_type=F32)
         for s in range(lo, hi):
+            kept[s] = part[:, (s - lo) * 128 : (s - lo + 1) * 128].reshape(2, ROWS // 2, 128)
+            pair_out[s] = kept[s, 1 - core].astype(BF16)
+            send(pair_out.at[s], pair_in.at[s], pair_send.at[s], pair_recv.at[s], sibling)
+
+    def pass_on(chunk):
+        for s in range(*CHUNKS[chunk]):
+            arrived(pair_in.at[s], pair_recv.at[s])
+            both = kept[s, core] + pair_in[s].astype(F32)
             if s == 0:
-                return part
+                return both
             m = MIRROR[s]
-            sum_out[s] = part[:, (s - lo) * 128 : (s - lo + 1) * 128].astype(BF16)
+            sum_out[s] = both.astype(BF16)
             send(sum_out.at[s], sum_in.at[m], sum_send.at[s], sum_recv.at[m], feat_dev(OFFS[s], q))
 
-    x_last(0)
     x_local(1, 2)
     x_wait(0)
     half(0, 0)
     x_local(3, 4)
-    x_last(1, 2)
     half(0, 1)
-    total = scores(0)
+    scores(0)
     x_local(5, 6)
-    x_last(3, 4)
     x_wait(1, 2)
     half(1, 0)
+    total = pass_on(0)
     x_local(7)
     half(1, 1)
     scores(1)
-    x_last(5, 6)
     x_wait(3, 4)
     half(2, 0)
-    x_last(7)
+    pass_on(1)
     half(2, 1)
     scores(2)
     x_wait(5, 6)
     half(3, 0)
+    pass_on(2)
     half(3, 1)
     scores(3)
     x_wait(7)
     half(4, 0)
+    pass_on(3)
     half(4, 1)
     scores(4)
 
@@ -204,21 +199,20 @@
         + lax.dot_general(ro_lo, x0, nt, preferred_element_type=F32)
     )
     linear = jnp.concatenate([linear, jnp.zeros((ROWS - classes, 128), F32)], axis=0)
+    pass_on(4)
 
     for s in range(1, 8):
         arrived(sum_in.at[s], sum_recv.at[s])
         total = total + sum_in[s].astype(F32)
-    loc[q] = total.astype(BF16)
-    mine = loc.at[q]
-    send(mine, mine, loc_send.at[2], loc_recv.at[2], neighbour)
-    send(mine, mine, loc_send.at[3], loc_recv.at[3], across)
-    send(mine, mine, loc_send.at[1], loc_recv.at[1], sibling)
-    arrived(loc.at[q_sib], loc_recv.at[1])
-    arrived(loc.at[q_x], loc_recv.at[2])
-    arrived(loc.at[3 - q], loc_recv.at[3])
-    total = loc[0].astype(F32)
+    loc[0] = total.astype(BF16)
+    send(loc.at[0], loc.at[2], loc_send.at[0], loc_recv.at[2], neighbour)
+    send(loc.at[0], loc.at[3], loc_send.at[1], loc_recv.at[3], across)
+    send(loc.at[0], loc.at[1], loc_send.at[2], loc_recv.at[1], sibling)
     for k in range(1, 4):
-        total = total + loc[k].astype(F32)
+        arrived(loc.at[k], loc_recv.at[k])
+    final[core] = loc[0].astype(F32) + loc[2].astype(F32)
+    final[1 - core] = loc[1].astype(F32) + loc[3].astype(F32)
+    total = final[...].reshape(ROWS, 128)
     rows = lax.broadcasted_iota(jnp.int32, (ROWS, 128), 0)
     inside = rows < classes
     value = jnp.where(inside, total * (1.0 / math.sqrt(feat_total)) + linear, -1e30)
@@ -247,13 +241,22 @@
         return jnp.dot(res_t[...], feats[:, cols], preferred_element_type=F32)
 
     back = [0] + [(k // 4) * 4 + (4 - k % 4) % 4 for k in range(1, 8)]
-
-    def grad_send_block(k):
-        grad_out[k] = grad_block(k).astype(BF16)
-        b = back[k]
-        send(grad_out.at[k], grad_in.at[b], grad_send.at[k], grad_recv.at[b], {"frames": frame_dev(k)})
-
-    grad_send_block(6)
+    opposite = {"frames": frame_dev(4)}
+
+    def grad_send_blocks(dy):
+        far, near = grad_block(4 + dy), grad_block(dy)
+        gx_out[dy] = far[:, :XF].astype(BF16)
+        send(gx_out.at[dy], gx_in.at[dy], gx_send.at[dy], gx_recv.at[dy], opposite)
+        kx[dy] = near[:, :XF]
+        if dy:
+            gy_out[dy, 0] = near[:, XF:].astype(BF16)
+            gy_out[dy, 1] = far[:, XF:].astype(BF16)
+            send(gy_out.at[dy], gy_in.at[4 - dy], gy_send.at[dy], gy_recv.at[4 - dy], {"frames": frame_dev(dy)})
+        else:
+            ky[0] = near[:, XF:]
+            ky[1] = far[:, XF:]
+
+    grad_send_blocks(2)
 
     ro_pad[...] = jnp.zeros_like(ro_pad)
     depth = x_all.shape[-1]
@@ -264,10 +267,23 @@
         b = back[k]
         send(ro_out, ro_in.at[b], ro_send.at[k], ro_recv.at[b], {"frames": frame_dev(k)})
 
-    for k in (5, 7, 2, 4, 1, 3):
-        grad_send_block(k)
-    own_grad = grad_block(0)
-
+    for dy in (1, 3, 0):
+        grad_send_blocks(dy)
+
+    def along_y(dy):
+        arrived(gx_in.at[dy], gx_recv.at[dy])
+        cy_out[dy] = (kx[dy] + gx_in[dy].astype(F32)).astype(BF16)
+        send(cy_out.at[dy], cy_in.at[4 - dy], cy_send.at[dy], cy_recv.at[4 - dy], {"frames": frame_dev(dy)})
+
+    along_y(2)
+    rest_own, rest_far = ky[0], ky[1]
+    for dy in (1, 3, 2):
+        arrived(gy_in.at[dy], gy_recv.at[dy])
+        rest_own = rest_own + gy_in[dy, 0].astype(F32)
+        rest_far = rest_far + gy_in[dy, 1].astype(F32)
+    cx[0] = rest_far.astype(BF16)
+    send(cx.at[0], cx.at[1], cx_send.at[0], cx_recv.at[0], opposite)
+    along_y(1)
     for k in range(1, 8):
         arrived(ro_in.at[k], ro_recv.at[k])
         ro_mine = ro_mine + ro_in[k].astype(F32)
@@ -276,14 +292,16 @@
     for s in range(1, 8):
         send(mine, mine, all_send.at[s], all_recv.at[MIRROR[s]], feat_dev(OFFS[s], q))
     send(mine, mine, all_pass.at[0], all_got.at[0], sibling)
-    for s in range(1, 8):
-        piece = ro_all.at[(z + OFFS[s] + 8) % 8, core]
-        arrived(piece, all_recv.at[s])
-        send(piece, piece, all_pass.at[s], all_got.at[s], sibling)
-
-    for k in (3, 1, 4, 2, 7, 5, 6):
-        arrived(grad_in.at[k], grad_recv.at[k])
-        own_grad = own_grad + grad_in[k].astype(F32)
+    along_y(3)
+
+    arrived(gx_in.at[0], gx_recv.at[0])
+    own_grad = kx[0] + gx_in[0].astype(F32)
+    arrived(cx.at[1], cx_recv.at[0])
+    rest_own = rest_own + cx[1].astype(F32)
+    for dy in (2, 1, 3):
+        arrived(cy_in.at[dy], cy_recv.at[dy])
+        own_grad = own_grad + cy_in[dy].astype(F32)
+    own_grad = jnp.concatenate([own_grad, rest_own], axis=1)
     cols = pl.ds(pl.multiple_of(group * cols_each, cols_each), cols_each)
     stepped = w[:, cols] - (5.0 / math.sqrt(batch)) * own_grad[:classes]
     trimmed = stepped - jnp.clip(stepped, -1.0, 1.0)
@@ -293,6 +311,10 @@
     for k in range(1, 8):
         b = back[k]
         send(norm_out, norm_in.at[b], norm_send.at[k], norm_recv.at[b], {"frames": frame_dev(k)})
+    for s in range(1, 8):
+        piece = ro_all.at[(z + OFFS[s] + 8) % 8, core]
+        arrived(piece, all_recv.at[s])
+        send(piece, piece, all_pass.at[s], all_got.at[s], sibling)
     for s in range(8):
         arrived(ro_all.at[(z + OFFS[s] + 8) % 8, 1 - core], all_got.at[s])
     for i in range(0, classes, 32):
@@ -328,7 +350,6 @@
         in_specs=[pl.BlockSpec(memory_space=pltpu.SMEM)] + [hbm] * 6,
         out_specs=(vmem, vmem),
         scratch_shapes=[
-            pltpu.VMEM((rows, depth), BF16),
             pltpu.VMEM((depth, columns), BF16),
             pltpu.VMEM((classes, columns), F32),
             pltpu.VMEM((8, 128), jnp.int32),
@@ -337,13 +358,24 @@
             pltpu.VMEM((ROWS, columns), BF16),
             pltpu.VMEM((8, 4, rows, depth), BF16),
             pltpu.VMEM((1024, columns), BF16),
-            pltpu.VMEM((8, ROWS, 128), BF16),
-            pltpu.VMEM((8, ROWS, 128), BF16),
-            pltpu.VMEM((4, ROWS, 128), BF16),
+            pltpu.VMEM((8, 2, ROWS // 2, 128), F32),
+            pltpu.VMEM((8, ROWS // 2, 128), BF16),
+            pltpu.VMEM((8, ROWS // 2, 128), BF16),
+            pltpu.VMEM((8, ROWS // 2, 128), BF16),
+            pltpu.VMEM((8, ROWS // 2, 128), BF16),
+            pltpu.VMEM((4, ROWS // 2, 128), BF16),
+            pltpu.VMEM((2, ROWS // 2, 128), F32),
             pltpu.VMEM((8, 2, ROWS // 2, 128), BF16),
             pltpu.VMEM((ROWS, 1024), BF16),
-            pltpu.VMEM((8, ROWS, each), BF16),
-            pltpu.VMEM((8, ROWS, each), BF16),
+            pltpu.VMEM((4, ROWS, XF), BF16),
+            pltpu.VMEM((4, ROWS, XF), BF16),
+            pltpu.VMEM((4, 2, ROWS, each - XF), BF16),
+            pltpu.VMEM((4, 2, ROWS, each - XF), BF16),
+            pltpu.VMEM((4, ROWS, XF), BF16),
+            pltpu.VMEM((4, ROWS, XF), BF16),
+            pltpu.VMEM((2, ROWS, each - XF), BF16),
+            pltpu.VMEM((4, ROWS, XF), F32),
+            pltpu.VMEM((2, ROWS, each - XF), F32),
             pltpu.VMEM((256, 512), F32),
             pltpu.VMEM((32, 256), BF16),
             pltpu.VMEM((8, 32, 256), BF16),
@@ -353,9 +385,13 @@
             dma((6,)),
             dma((32,)), dma((8, 4)),
             dma((8,)), dma((8,)),
+            dma((8,)), dma((8,)),
+            dma((3,)), dma((4,)),
+            dma((8,)), dma((8,)), dma((8,)), dma((8,)),
             dma((4,)), dma((4,)),
-            dma((8,)), dma((8,)), dma((8,)), dma((8,)),
-            dma((8,)), dma((8,)),
+            dma((4,)), dma((4,)),
+            dma((4,)), dma((4,)),
+            dma((1,)), dma((1,)),
             dma((8,)), dma((8,)),
             dma((8,)), dma((8,)), dma((8,)), dma((8,)),
             dma((8,)), dma((8,)),

time: 77.5 us -> 74 us (0.955); the launches traced: 76.5 us -> 73.9 us
  Pallas kernels: 73.7 us -> 71.2 us
    pallas_call x1, Pallas kernels: 73.7 us -> 71.2 us  [body(): pl.pallas_call(functools.partial(kernel, batch, columns * n_feat, classes...]
where the time goes in v4:
time: 74 us; the launch traced here: 73.9 us
  Pallas kernels  71.2 us (96%)
  local copies, waits for them, and re-layouts  1.44 us (2%)
  between operations  1.29 us (2%)
    pallas_call x1, Pallas kernels, body(): pl.pallas_call(functools.partial(kernel, batch, columns * n_feat, classes...  71.2 us

profile of v4, /device:TPU:1, one launch (start us, length us, event | category | flops | bytes accessed | tf_op | source)
XLA Modules:
  0.0 73.9 jit_solution(9733463151594352627)
XLA Ops:
  1.3 71.2 %fourier_step.1 = (f32[147,512]{1,0:T(8,128)S(1)}, f32[147,440]{1,0:T(8,128)S(1)}) custom-call(f32[1]{0:T(128)S(6)} %copy.13.scale_ref, bf16[32,440]{1,0:T(8,128)(2,1)} %x_hbm.1, bf16[440,4096]{1,0:T(8,128)(2,1)} %proj_hbm.1, f32[147,4096]{1,0:T(8,128)} %w_hbm.1, s32[8,128]{1,0:T(8,128)} %bitcast.3, f32[1,4096]{1,0:T(1,128)} %bitcast.2, f32[147,440]{1,0:T(8,128)} %readout_hbm.1), custom_call_target="tpu_custom_call" | custom-call | tf_op jit(solution)/shard_map/fourier_step/pallas_call | solution.py:344
  72.5 0.7 copy.11
  73.2 0.7 copy.12

commit v5 on v4

--- a/solution.py
+++ b/solution.py
@@ -37,7 +37,7 @@
     out_ref, readout_out_ref,
     proj, w, labels, shift, readout, w_low, x_all, feats, kept, pair_out, pair_in, sum_out, sum_in, loc, final, res_all, res_t,
     gx_out, gx_in, gy_out, gy_in, cy_out, cy_in, cx, kx, ky, ro_pad, ro_out, ro_in, ro_all, norm_out, norm_in,
-    local_sem, x_send, x_recv, pair_send, pair_recv, sum_send, sum_recv, loc_send, loc_recv, res_send, res_recv, res_pass, res_got,
+    local_sem, far_z, far_x, x_send, x_recv, pair_send, pair_recv, sum_send, sum_recv, loc_send, loc_recv, res_send, res_recv, res_pass, res_got,
     gx_send, gx_recv, gy_send, gy_recv, cy_send, cy_recv, cx_send, cx_recv, ro_send, ro_recv, all_send, all_recv, all_pass, all_got, norm_send, norm_recv,
 ):
     me = lax.axis_index("feat")
@@ -80,11 +80,14 @@
         copy.start()
 
     barrier = pltpu.get_barrier_semaphore()
-    partners = [feat_dev(d, q) for d in OFFS[1:]] + [neighbour, across, sibling]
-    partners += [{"frames": frame_dev(k)} for k in range(1, 8)]
+    partners = [feat_dev(d, q) for d in OFFS[1:5]] + [neighbour, across, sibling]
+    partners += [{"frames": frame_dev(k)} for k in range(1, 5)]
     for dev in partners:
         pl.semaphore_signal(barrier, inc=1, device_id=dev, device_id_type=MESH)
     pl.semaphore_wait(barrier, len(partners))
+    for d in (2, -2):
+        pl.semaphore_signal(far_z, inc=1, device_id=feat_dev(d, q), device_id_type=MESH)
+    pl.semaphore_signal(far_x, inc=1, device_id={"frames": frame_dev(4)}, device_id_type=MESH)
 
     def gather_local(s):
         piece = x_all.at[s, q]
@@ -109,13 +112,19 @@
             gather_wait(s)
 
     gather_local(0)
-    for s in range(1, 8):
-        m = MIRROR[s]
-        send(x_hbm, x_all.at[m, q], x_send.at[s], x_recv.at[m, 0], feat_dev(OFFS[s], q))
+
+    def gather_z(slots):
+        for s in slots:
+            m = MIRROR[s]
+            send(x_hbm, x_all.at[m, q], x_send.at[s], x_recv.at[m, 0], feat_dev(OFFS[s], q))
+
+    gather_z((1, 2, 3, 4))
 
     w_low[144:ROWS, :] = jnp.zeros((ROWS - 144, w_low.shape[1]), BF16)
     local[3].wait()
     w_low[0:classes, :] = w[...].astype(BF16)
+    pl.semaphore_wait(far_z, 2)
+    gather_z((5, 6, 7))
     local[1].wait()
     local[2].wait()
     local[0].wait()
@@ -258,6 +267,7 @@
 
     grad_send_blocks(2)
 
+    pl.semaphore_wait(far_x, 1)
     ro_pad[...] = jnp.zeros_like(ro_pad)
     depth = x_all.shape[-1]
     ro_pad[0:ROWS, 0:depth] = jnp.dot(res_t[...], x_all[...].reshape(1024, depth), preferred_element_type=F32)
@@ -383,6 +393,8 @@
             pltpu.VMEM((8, 128), F32),
             pltpu.VMEM((8, 8, 128), F32),
             dma((6,)),
+            pltpu.SemaphoreType.REGULAR,
+            pltpu.SemaphoreType.REGULAR,
             dma((32,)), dma((8, 4)),
             dma((8,)), dma((8,)),
             dma((8,)), dma((8,)),

time: 74 us -> 73.1 us (0.988)
  Pallas kernels: 71.2 us -> 70.3 us
    pallas_call x1, Pallas kernels: 71.2 us -> 70.3 us  [body(): pl.pallas_call(functools.partial(kernel, batch, columns * n_feat, classes...]
where the time goes in v5:
time: 73.1 us
  Pallas kernels  70.3 us (96%)
  local copies, waits for them, and re-layouts  1.44 us (2%)
  between operations  1.29 us (2%)
    pallas_call x1, Pallas kernels, body(): pl.pallas_call(functools.partial(kernel, batch, columns * n_feat, classes...  70.3 us

profile of v5, /device:TPU:1, one launch (start us, length us, event | category | flops | bytes accessed | tf_op | source)
XLA Modules:
  0.0 73.1 jit_solution(12076952165492670449)
XLA Ops:
  1.3 70.3 %fourier_step.1 = (f32[147,512]{1,0:T(8,128)S(1)}, f32[147,440]{1,0:T(8,128)S(1)}) custom-call(f32[1]{0:T(128)S(6)} %copy.13.scale_ref, bf16[32,440]{1,0:T(8,128)(2,1)} %x_hbm.1, bf16[440,4096]{1,0:T(8,128)(2,1)} %proj_hbm.1, f32[147,4096]{1,0:T(8,128)} %w_hbm.1, s32[8,128]{1,0:T(8,128)} %bitcast.3, f32[1,4096]{1,0:T(1,128)} %bitcast.2, f32[147,440]{1,0:T(8,128)} %readout_hbm.1), custom_call_target="tpu_custom_call" | custom-call | tf_op jit(solution)/shard_map/fourier_step/pallas_call | solution.py:354
  71.6 0.7 copy.11
  72.3 0.7 copy.12

commit v6 on v5

--- a/solution.py
+++ b/solution.py
@@ -89,11 +89,23 @@
         pl.semaphore_signal(far_z, inc=1, device_id=feat_dev(d, q), device_id_type=MESH)
     pl.semaphore_signal(far_x, inc=1, device_id={"frames": frame_dev(4)}, device_id_type=MESH)
 
+    def half_of(piece, h):
+        return piece.at[16 * h : 16 * h + 16]
+
     def gather_local(s):
         piece = x_all.at[s, q]
         source = piece if s else x_hbm
-        if s:
+        if s == 7:
+            for h in range(2):
+                arrived(half_of(piece, h), x_recv.at[7 - 7 * h, 0])
+        elif s:
             arrived(piece, x_recv.at[s, 0])
+        if s in (3, 4):
+            on = -1 if s == 3 else 1
+            send(piece, x_all.at[s + 2, q], x_send.at[s + 2], x_recv.at[s + 2, 0], feat_dev(on, q))
+            h = s - 3
+            end = half_of(x_all.at[7, q], h)
+            send(half_of(piece, h), end, x_send.at[7 * h], x_recv.at[7 - 7 * h, 0], feat_dev(2 * on, q))
         send(source, piece, x_send.at[8 + s], x_recv.at[s, 2], neighbour)
         send(source, piece, x_send.at[24 + s], x_recv.at[s, 3], across)
         send(source, piece, x_send.at[16 + s], x_recv.at[s, 1], sibling)
@@ -112,19 +124,13 @@
             gather_wait(s)
 
     gather_local(0)
-
-    def gather_z(slots):
-        for s in slots:
-            m = MIRROR[s]
-            send(x_hbm, x_all.at[m, q], x_send.at[s], x_recv.at[m, 0], feat_dev(OFFS[s], q))
-
-    gather_z((1, 2, 3, 4))
+    for s in (1, 2, 3, 4):
+        m = MIRROR[s]
+        send(x_hbm, x_all.at[m, q], x_send.at[s], x_recv.at[m, 0], feat_dev(OFFS[s], q))
 
     w_low[144:ROWS, :] = jnp.zeros((ROWS - 144, w_low.shape[1]), BF16)
     local[3].wait()
     w_low[0:classes, :] = w[...].astype(BF16)
-    pl.semaphore_wait(far_z, 2)
-    gather_z((5, 6, 7))
     local[1].wait()
     local[2].wait()
     local[0].wait()
@@ -165,17 +171,15 @@
             sum_out[s] = both.astype(BF16)
             send(sum_out.at[s], sum_in.at[m], sum_send.at[s], sum_recv.at[m], feat_dev(OFFS[s], q))
 
-    x_local(1, 2)
     x_wait(0)
     half(0, 0)
-    x_local(3, 4)
+    x_local(1, 2, 3, 4)
     half(0, 1)
     scores(0)
-    x_local(5, 6)
     x_wait(1, 2)
     half(1, 0)
     total = pass_on(0)
-    x_local(7)
+    x_local(5, 6, 7)
     half(1, 1)
     scores(1)
     x_wait(3, 4)
@@ -186,6 +190,7 @@
     x_wait(5, 6)
     half(3, 0)
     pass_on(2)
+    pl.semaphore_wait(far_z, 2)
     half(3, 1)
     scores(3)
     x_wait(7)

time: 73.1 us -> 72.9 us (level)
  no operation moved by 1% of the time
where the time goes in v6:
time: 72.9 us; the launch traced here: 72.6 us
  Pallas kernels  69.8 us (96%)
  local copies, waits for them, and re-layouts  1.44 us (2%)
  between operations  1.29 us (2%)
    pallas_call x1, Pallas kernels, body(): pl.pallas_call(functools.partial(kernel, batch, columns * n_feat, classes...  69.8 us

profile of v6, /device:TPU:1, one launch (start us, length us, event | category | flops | bytes accessed | tf_op | source)
XLA Modules:
  0.0 72.6 jit_solution(14212681067689704012)
XLA Ops:
  1.3 69.8 %fourier_step.1 = (f32[147,512]{1,0:T(8,128)S(1)}, f32[147,440]{1,0:T(8,128)S(1)}) custom-call(f32[1]{0:T(128)S(6)} %copy.13.scale_ref, bf16[32,440]{1,0:T(8,128)(2,1)} %x_hbm.1, bf16[440,4096]{1,0:T(8,128)(2,1)} %proj_hbm.1, f32[147,4096]{1,0:T(8,128)} %w_hbm.1, s32[8,128]{1,0:T(8,128)} %bitcast.3, f32[1,4096]{1,0:T(1,128)} %bitcast.2, f32[147,440]{1,0:T(8,128)} %readout_hbm.1), custom_call_target="tpu_custom_call" | custom-call | tf_op jit(solution)/shard_map/fourier_step/pallas_call | solution.py:359
  71.1 0.7 copy.11
  71.8 0.7 copy.12

commit v7 on v6

--- a/solution.py
+++ b/solution.py
@@ -272,6 +272,8 @@
 
     grad_send_blocks(2)
 
+    grad_send_blocks(1)
+    grad_send_blocks(3)
     pl.semaphore_wait(far_x, 1)
     ro_pad[...] = jnp.zeros_like(ro_pad)
     depth = x_all.shape[-1]
@@ -281,9 +283,7 @@
     for k in range(1, 8):
         b = back[k]
         send(ro_out, ro_in.at[b], ro_send.at[k], ro_recv.at[b], {"frames": frame_dev(k)})
-
-    for dy in (1, 3, 0):
-        grad_send_blocks(dy)
+    grad_send_blocks(0)
 
     def along_y(dy):
         arrived(gx_in.at[dy], gx_recv.at[dy])
@@ -299,6 +299,7 @@
     cx[0] = rest_far.astype(BF16)
     send(cx.at[0], cx.at[1], cx_send.at[0], cx_recv.at[0], opposite)
     along_y(1)
+    along_y(3)
     for k in range(1, 8):
         arrived(ro_in.at[k], ro_recv.at[k])
         ro_mine = ro_mine + ro_in[k].astype(F32)
@@ -307,7 +308,6 @@
     for s in range(1, 8):
         send(mine, mine, all_send.at[s], all_recv.at[MIRROR[s]], feat_dev(OFFS[s], q))
     send(mine, mine, all_pass.at[0], all_got.at[0], sibling)
-    along_y(3)
 
     arrived(gx_in.at[0], gx_recv.at[0])
     own_grad = kx[0] + gx_in[0].astype(F32)

time: 72.9 us -> 71.9 us (0.986)
  Pallas kernels: 69.8 us -> 68.8 us
    pallas_call x1, Pallas kernels: 69.8 us -> 68.8 us  [body(): pl.pallas_call(functools.partial(kernel, batch, columns * n_feat, classes...]
where the time goes in v7:
time: 71.9 us; the launch traced here: 71.6 us
  Pallas kernels  68.8 us (96%)
  local copies, waits for them, and re-layouts  1.44 us (2%)
  between operations  1.29 us (2%)
    pallas_call x1, Pallas kernels, body(): pl.pallas_call(functools.partial(kernel, batch, columns * n_feat, classes...  68.8 us
    unnamed x2, local copies, waits for them, and re-layouts  1.44 us

profile of v7, /device:TPU:1, one launch (start us, length us, event | category | flops | bytes accessed | tf_op | source)
XLA Modules:
  0.0 71.6 jit_solution(5324053017302421129)
XLA Ops:
  1.3 68.8 %fourier_step.1 = (f32[147,512]{1,0:T(8,128)S(1)}, f32[147,440]{1,0:T(8,128)S(1)}) custom-call(f32[1]{0:T(128)S(6)} %copy.13.scale_ref, bf16[32,440]{1,0:T(8,128)(2,1)} %x_hbm.1, bf16[440,4096]{1,0:T(8,128)(2,1)} %proj_hbm.1, f32[147,4096]{1,0:T(8,128)} %w_hbm.1, s32[8,128]{1,0:T(8,128)} %bitcast.3, f32[1,4096]{1,0:T(1,128)} %bitcast.2, f32[147,440]{1,0:T(8,128)} %readout_hbm.1), custom_call_target="tpu_custom_call" | custom-call | tf_op jit(solution)/shard_map/fourier_step/pallas_call | solution.py:359
  70.1 0.7 %copy.11 = f32[147,512]{1,0:T(8,128)} copy(f32[147,512]{1,0:T(8,128)S(1)} %get-tuple-element.2) | data formatting | bytes 602112
  70.9 0.7 %copy.12 = f32[147,440]{1,0:T(8,128)} copy(f32[147,440]{1,0:T(8,128)S(1)} %get-tuple-element.3) | data formatting | bytes 517440
